TPU v7x, 512 devices: a whole 4x8x8 slice. The times are simulated.
512 devices in a mesh: dp: 2 (over x_hi), ctx: 32 (over x_lo, y, core), head: 8 (over z).
Axes of the slice: x: 4 (x_hi: 2, x_lo: 2; x = x_hi * 2 + x_lo), y: 8, z: 8, core: 2. Of those that a mesh axis runs over, the one named last changes fastest.
Arguments:
- query_latent_rows: bfloat16 [2, 4096, 1536], P('dp', 'ctx'), may hold values from -6 to 6
- latent: bfloat16 [2, 4096, 576], P('dp', 'ctx'), may hold values from -6 to 6
- wq_b: bfloat16 [48, 1536, 192], P('head', 'ctx'), may hold values from -5 to 5
- key_up_weight: bfloat16 [48, 512, 128], P('head', 'ctx'), may hold values from -0.5 to 0.5
- value_up_weight: bfloat16 [48, 512, 128], P('head', 'ctx'), may hold values from -0.25 to 0.25
- tau: int32 [48], P('head'), may hold values from 1 to 2
Outputs:
- attention: bfloat16 [2, 4096, 6144], P('dp', 'ctx', 'head')
- new_wq: bfloat16 [48, 1536, 192], P('head', 'ctx')
- new_uk: bfloat16 [48, 512, 128], P('head', 'ctx')
All inputs are finite; a program needn't handle non-finite values.
Results may differ from a plain program's by a relative error of at most 0.017.
The roundings to bfloat16 on the way count: a program that leaves them out, or rounds other values in their place, can miss the bound.
Values may be sent and summed in bfloat16 or wider, within the bound.
A program may use at most 64 MiB of HBM per device.

v0:
```python
import jax
import jax.numpy as jnp
from jax import lax
from jax.sharding import PartitionSpec as P


def rotate(value_rows, positions):
    half = value_rows.shape[-1] // 2
    freq = 50000.0 ** (-2.0 * jnp.arange(half, dtype=jnp.float32) / value_rows.shape[-1])
    angle = positions.astype(jnp.float32)[:, None] * freq[None, :]
    cosine = jnp.cos(angle)[:, None, :]
    sine = jnp.sin(angle)[:, None, :]
    first = value_rows[..., :half]
    second = value_rows[..., half:]
    return jnp.concatenate([first * cosine - second * sine, second * cosine + first * sine], -1)


def shards(query_latent_rows, latent, wq_b, key_up_weight, value_up_weight, tau):
    tok_rows = query_latent_rows.shape[1]
    heads_here = wq_b.shape[0]
    qk_width = wq_b.shape[2]
    nope_width = key_up_weight.shape[2]
    value_width = value_up_weight.shape[2]
    own_rows = query_latent_rows[0]
    query = jnp.einsum(
        "tr,hrc->thc",
        own_rows,
        lax.all_gather(wq_b, "ctx", axis=1, tiled=True),
        preferred_element_type=jnp.float32,
    )
    key_up, value_up_rows = (
        lax.all_gather(key_up_weight, "ctx", axis=1, tiled=True),
        lax.all_gather(value_up_weight, "ctx", axis=1, tiled=True),
    )
    kv_width = key_up.shape[1]
    positions = lax.axis_index("ctx") * tok_rows + jnp.arange(tok_rows, dtype=jnp.int32)
    q_nope = query[..., :nope_width].astype(jnp.bfloat16)
    q_lat = jnp.einsum("thn,hkn->thk", q_nope, key_up, preferred_element_type=jnp.float32)
    q_rot = rotate(query[..., nope_width:], positions)
    q_full = (jnp.concatenate([q_lat, q_rot], -1) * qk_width ** (-0.5)).astype(jnp.bfloat16)
    running = jnp.full((tok_rows, heads_here), -1e30, jnp.float32)
    key_rows = lax.all_gather(latent, "ctx", axis=1, tiled=True)[0]
    score = jnp.einsum("thc,kc->thk", q_full, key_rows, preferred_element_type=jnp.float32)
    key_pos = jnp.arange(key_rows.shape[0], dtype=jnp.int32)
    mask = key_pos[None, None, :] <= positions[:, None, None]
    score = jnp.where(mask, score, jnp.float32(-1e30))
    fresh = jnp.maximum(running, jnp.max(score, -1))
    exponent_terms = jnp.where(mask, jnp.exp(score - fresh[..., None]), jnp.float32(0.0))
    totals = jnp.sum(exponent_terms, -1)
    summed = jnp.einsum(
        "thk,kc->thc",
        exponent_terms.astype(jnp.bfloat16),
        key_rows[:, :kv_width],
        preferred_element_type=jnp.float32,
    )
    running, totals, summed = (fresh, totals, summed)
    mixed_output = (summed / totals[..., None]).astype(jnp.bfloat16)
    attention = jnp.einsum(
        "euz,uzo->euo", mixed_output, value_up_rows, preferred_element_type=jnp.float32
    ).astype(jnp.bfloat16)
    attention = attention.reshape(1, tok_rows, heads_here * value_width)
    peak = lax.pmax(jnp.max(running, 0), ("dp", "ctx"))
    limit = tau.astype(jnp.float32)
    gamma = limit / jnp.maximum(peak, limit)
    root = jnp.sqrt(gamma)
    wq_wide = wq_b.astype(jnp.float32)
    new_wq = jnp.concatenate(
        [
            wq_wide[..., :nope_width] * root[:, None, None],
            wq_wide[..., nope_width:] * gamma[:, None, None],
        ],
        -1,
    ).astype(jnp.bfloat16)
    new_uk = (key_up_weight.astype(jnp.float32) * root[:, None, None]).astype(jnp.bfloat16)
    return (attention, new_wq, new_uk)


def solution(mesh):
    in_specs = (
        P("dp", "ctx", None),
        P("dp", "ctx", None),
        P("head", "ctx", None),
        P("head", "ctx", None),
        P("head", "ctx", None),
        P("head"),
    )
    out_specs = (P("dp", "ctx", "head"), P("head", "ctx", None), P("head", "ctx", None))
    return jax.shard_map(shards, mesh=mesh, in_specs=in_specs, out_specs=out_specs, check_vma=False)
```

profile of v0, /device:TPU:1, one launch (start us, length us, event | category | flops | bytes accessed | tf_op | source)
XLA Modules:
  0.0 320.3 jit_solution(1628036058542375703)
XLA Ops:
  7.2 0.0 copy-start
  7.2 0.0 all-gather.3.cloned.1.call-start
  7.2 0.7 all-gather.3.cloned.1.call-update
  7.9 0.0 all-gather.5.cloned.1.call-start
  8.0 0.7 all-gather.5.cloned.1.call-update
  8.7 1.6 convert_element_type.42
  10.3 0.1 multiply_cosine_fusion
  10.5 40.0 %all_gather.13 = bf16[6,512,128]{2,1,0:T(8,128)(2,1)S(1)} all-gather(bf16[6,16,128]{2,1,0:T(8,128)(2,1)} %param.9), channel_id=1, replica_groups=mesh['dp'=2,'ctx'=32,'head'=8] {'ctx'}, dimensions={1}, use_global_device_ids=true | all-gather | bytes 811008 | tf_op jit(solution)/shard_map/all_gather | solution.py:32
  50.5 37.7 %all_gather.15 = bf16[6,512,128]{2,1,0:T(8,128)(2,1)} all-gather(bf16[6,16,128]{2,1,0:T(8,128)(2,1)} %param.10), channel_id=1, replica_groups=mesh['dp'=2,'ctx'=32,'head'=8] {'ctx'}, dimensions={1}, use_global_device_ids=true | all-gather | bytes 811008 | tf_op jit(solution)/shard_map/all_gather | solution.py:33
  88.1 0.4 iota_compare_fusion
  88.5 0.0 all-gather.3.cloned.1.call-done
  88.5 0.0 copy-done
  88.6 4.1 %fusion.18 = f32[128,6,192]{0,2,1:T(8,128)S(1)} fusion(bf16[6,1536,192]{2,1,0:T(8,128)(2,1)} %all-gather.3.cloned.1.call-done, bf16[1,128,1536]{2,1,0:T(8,128)(2,1)S(1)} %copy-done), kind=kOutput, calls=%fused_computation.21 | convolution fusion | flops 452984832 | bytes 4521984 | tf_op jit(solution)/shard_map/tr,hrc->thc/dot_general | solution.py:25
  92.7 0.3 convolution_bitcast_fusion
  93.1 72.5 %all-gather.5.cloned.1.call-done = bf16[1,4096,576]{1,2,0:T(8,128)(2,1)} async-done(((bf16[1,128,576]{1,2,0:T(8,128)(2,1)}), bf16[1,4096,576]{1,2,0:T(8,128)(2,1)}) %all-gather.5.cloned.1.call-update) | async-done | bytes 4718608 | tf_op jit(solution)/shard_map/all_gather | solution.py:42
  165.6 7.6 %select_reduce_fusion = (f32[128,6]{0,1:T(8,128)S(1)}, f32[128,6,4096]{2,0,1:T(8,128)S(1)}) fusion(pred[128,4096]{1,0:T(8,128)(4,1)S(1)} %iota_compare_fusion, bf16[1,4096,576]{1,2,0:T(8,128)(2,1)} %all-gather.5.cloned.1.call-done, f32[128,6,32]{0,2,1:T(8,128)S(1)} %get-tuple-element.9, f32[128,6,32]{0,2,1:T(8,128)S(1)} %get-tuple-element.8, ...), kind=kOutput, calls=%fused_computation.1 | convolution fusion | flops 3631938816 | bytes 19598336 | tf_op jit(solution)/shard_map/thc,kc->thk/dot_general | solution.py:43
  173.3 0.0 copy-start.1
  173.3 0.1 fusion.29
  173.4 0.0 copy-start.3
  173.4 3.9 %fusion = f32[128,6]{0,1:T(8,128)S(1)} fusion(f32[128,6,4096]{2,0,1:T(8,128)S(1)} %get-tuple-element.15, f32[128,6]{0,1:T(8,128)S(1)} %get-tuple-element.11, pred[128,4096]{1,0:T(8,128)(4,1)S(1)} %iota_compare_fusion), kind=kLoop, calls=%fused_computation.2 | loop fusion | flops 12582144 | bytes 13113344 | tf_op jit(solution)/shard_map/reduce_sum | solution.py:49
  177.3 0.5 copy-done.1
  177.8 0.0 copy-done.3
  177.8 9.6 %convolution_convert_fusion = bf16[6,128,128]{1,2,0:T(8,128)(2,1)S(1)} fusion(bf16[6,512,128]{2,1,0:T(8,128)(2,1)S(1)} %copy-done.3, bf16[4096,576]{0,1:T(8,128)(2,1)} %bitcast.27, f32[128,6,4096]{2,0,1:T(8,128)} %copy-done.1, f32[128,6]{0,1:T(8,128)S(1)} %get-tuple-element.11, pred[128,4096]{1,0:T(8,128)(4,1)S(1)} %iota_compare_fusion, f32[128,6]{0,1:T(8,128)S(1)} %fusion), kind=kOutput, calls=%fused_computation.17 | convolution fusion | flops 3335356416 | bytes 18290688 | tf_op jit(solution)/shard_map/euz,uzo->euo/dot_general | solution.py:58
  187.4 0.8 copy.9
  188.2 123.7 %pmax.7 = f32[6]{0:T(128)S(1)} all-reduce(f32[6]{0:T(128)S(1)} %get-tuple-element.10), channel_id=1, replica_groups=mesh['dp'=2,'ctx'=32,'head'=8] {'dp','ctx'}, use_global_device_ids=true, to_apply=%region_3.4 | all-reduce | flops 6 | bytes 48 | tf_op jit(solution)/shard_map/pmax | solution.py:62
  311.9 0.0 copy-done.5
  311.9 0.0 copy-done.4
  311.9 0.7 multiply_convert_fusion
  312.6 0.0 copy-done.2
  312.6 0.1 fusion.21
  312.7 0.1 fusion.20
  312.8 0.7 pad_maximum_fusion
  (8 shorter events, 0.1 us)
Async XLA Ops:
  7.2 81.4 %copy-start = (bf16[1,128,1536]{2,1,0:T(8,128)(2,1)S(1)}, bf16[1,128,1536]{2,1,0:T(8,128)(2,1)}, u32[]{:S(2)}) copy-start(bf16[1,128,1536]{2,1,0:T(8,128)(2,1)} %param.6) | copy-start | bytes 1179652
  7.2 81.4 %all-gather.3.cloned.1.call-start = ((), (), s32[]{:S(2)}) async-start(), calls=%async_computation | async-start | bytes 4866048 | tf_op jit(solution)/shard_map/all_gather | solution.py:28
  7.9 157.7 %all-gather.5.cloned.1.call-start = ((), (), s32[]{:S(2)}) async-start(), calls=%async_computation.1 | async-start | bytes 4866048 | tf_op jit(solution)/shard_map/all_gather | solution.py:42
  173.3 4.5 %copy-start.1 = (f32[128,6,4096]{2,0,1:T(8,128)}, f32[128,6,4096]{2,0,1:T(8,128)S(1)}, u32[]{:S(2)}) copy-start(f32[128,6,4096]{2,0,1:T(8,128)S(1)} %get-tuple-element.15) | copy-start | bytes 37748740
  173.4 4.4 %copy-start.3 = (bf16[6,512,128]{2,1,0:T(8,128)(2,1)S(1)}, bf16[6,512,128]{2,1,0:T(8,128)(2,1)}, u32[]{:S(2)}) copy-start(bf16[6,512,128]{2,1,0:T(8,128)(2,1)} %all_gather.15) | copy-start | bytes 2359300
  177.8 134.1 %copy-start.5 = (s32[6]{0:T(128)S(1)}, s32[6]{0:T(128)}, u32[]{:S(2)}) copy-start(s32[6]{0:T(128)} %param.11) | copy-start | bytes 76
  177.8 134.1 %copy-start.4 = (bf16[6,16,128]{2,1,0:T(8,128)(2,1)S(1)}, bf16[6,16,128]{2,1,0:T(8,128)(2,1)}, u32[]{:S(2)}) copy-start(bf16[6,16,128]{2,1,0:T(8,128)(2,1)} %param.9) | copy-start | bytes 73732
  177.8 134.8 %copy-start.2 = (f32[6,48,192]{2,1,0:T(8,128)S(1)}, f32[6,48,192]{2,1,0:T(8,128)}, u32[]{:S(2)}) copy-start(f32[6,48,192]{2,1,0:T(8,128)} %convert_element_type.42) | copy-start | bytes 663556
Sparse Core Ops, SparseCore 0:
  10.1 76.6 all-gather.2
  88.9 76.6 all-gather.4
where the time goes:
time: 323 us; the launch traced here: 320 us
  blocking collectives  201 us (62%)
  waiting for transfers between devices  73.9 us (23%)
  matrix products  21.7 us (7%)
  between operations  14.2 us (4%)
  other arithmetic  7.78 us (2%)
    pmax x1, blocking collectives, shards(): peak = lax.pmax(jnp.max(running, 0), ('dp', 'ctx'))  124 us
    all_gather x1, waiting for transfers between devices, shards(): key_rows = lax.all_gather(latent, 'ctx', axis=1, tiled=True)[0]  72.5 us
    all_gather x1, blocking collectives, shards(): lax.all_gather(key_up_weight, 'ctx', axis=1, tiled=True)  40 us
    all_gather x1, blocking collectives, shards(): lax.all_gather(value_up_weight, 'ctx', axis=1, tiled=True)  37.7 us
    dot_general x1, matrix products, shards(): jnp.einsum('euz,uzo->euo', mixed_output, value_up_rows, preferred_element...  9.58 us
    dot_general x1, matrix products, shards(): jnp.einsum('thc,kc->thk', q_full, key_rows, preferred_element_type=jnp.fl...  7.65 us
  transfers between devices with their start and end apart: 2, of which 1 were waited for; matrix products, arithmetic and copies ran while one was open for 2% of the time, Pallas kernels for 0%

commit v1 on v0

v1 whole, which is shorter than its diff:
```python
import functools

import jax
import jax.numpy as jnp
from jax import lax
from jax.experimental import pallas as pl
from jax.experimental.pallas import tpu as pltpu
from jax.sharding import PartitionSpec as P

MESH = pl.DeviceIdType.MESH
F32 = jnp.float32
BF16 = jnp.bfloat16
LOW = -1e30

HEADS = 6
ROWS = 128
NOPE = 128
ROT = 64
LAT = 512
KEYW = 640
RING = 8
CHIPS = 16
GROUP = 4
GROUPS = CHIPS // GROUP
SLICE = ROWS // RING
WQW = HEADS * (NOPE + ROT)
UPW = HEADS * NOPE
QROWS = HEADS * ROWS
CHUNK = 2


def kernel(
    x_ref, lat_ref, wq_ref, uk_ref, uv_ref, tau_ref,
    att_ref, nwq_ref, nuk_ref,
    wq, uk, uv, keys, qf, mx, tot, acc, pk,
    l1_s, l1_r, wy_s, wy_r, wx_s, wx_r, ws_s, ws_r, z_s, z_r, ks_s, ks_r, pk_s, pk_r,
):
    dp = lax.axis_index("dp")
    ctx = lax.axis_index("ctx")
    z = lax.axis_index("head")
    core = lax.rem(ctx, 2)
    chip = ctx // 2
    xlo = chip // RING
    y = lax.rem(chip, RING)

    def wrap(v):
        return lax.rem(v + 2 * RING, RING)

    def dev(d, xl, yy, c, zz):
        return (d, (xl * RING + yy) * 2 + c, zz)

    sibling = dev(dp, xlo, y, 1 - core, z)
    y_next = (dev(dp, xlo, wrap(y + 1), core, z), dev(dp, xlo, wrap(y - 1), core, z))
    z_next = (dev(dp, xlo, y, core, wrap(z + 1)), dev(dp, xlo, y, core, wrap(z - 1)))
    x_up = dev(lax.rem(dp + xlo, 2), 1 - xlo, y, core, z)
    x_down = dev(lax.rem(dp + 1 + xlo, 2), 1 - xlo, y, core, z)

    def l1_dev(dx, dy):
        return dev(dp, lax.rem(xlo + dx, 2), wrap(y + dy), core, z)

    def plane_dev(k):
        return dev(
            lax.rem(dp + k // 4, 2), lax.rem(xlo + (k // 2) % 2, 2), y, lax.rem(core + k % 2, 2), z
        )

    barrier = pltpu.get_barrier_semaphore()
    partners = [l1_dev(dx, dy) for dx in range(2) for dy in range(RING) if dx or dy]
    partners += [plane_dev(k) for k in range(1, 8) if k != 2]
    partners += list(z_next)
    for partner in partners:
        pl.semaphore_signal(barrier, inc=1, device_id=partner, device_id_type=MESH)

    for h in range(HEADS):
        wq[chip, core, :, h * NOPE : (h + 1) * NOPE] = wq_ref[h, :, :NOPE]
        uk[chip, core, :, h * NOPE : (h + 1) * NOPE] = uk_ref[h]
        uv[chip, core, :, h * NOPE : (h + 1) * NOPE] = uv_ref[h]
    for j in range(HEADS // 2):
        pair = jnp.concatenate([wq_ref[2 * j, :, NOPE:], wq_ref[2 * j + 1, :, NOPE:]], -1)
        wq[chip, core, :, UPW + j * 128 : UPW + (j + 1) * 128] = pair
    own_rows = pl.ds(pl.multiple_of(z * SLICE, SLICE), SLICE)
    own_slice = lat_ref[0, own_rows, :]
    keys[chip, core, own_rows, :] = jnp.concatenate(
        [own_slice, jnp.zeros((SLICE, KEYW - LAT - ROT), BF16)], -1
    )

    pl.semaphore_wait(barrier, len(partners))

    sent = []

    def guarded(cond, f):
        if cond is None:
            f()
        else:
            pl.when(cond)(f)

    def send(make, cond=None):
        sent.append((cond, make))
        guarded(cond, lambda: make().start())

    def arrive(make, cond=None):
        guarded(cond, lambda: make().wait_recv())

    def copy(ref, ssem, rsem, to):
        return lambda: pltpu.make_async_remote_copy(
            src_ref=ref(), dst_ref=ref(), send_sem=ssem, recv_sem=rsem, device_id=to, device_id_type=MESH
        )

    def slice_of(p0, n, zz):
        rows = pl.ds(pl.multiple_of(zz * SLICE, SLICE), SLICE)
        return keys.at[pl.ds(p0, n), core, rows, :]

    my_group = chip // GROUP
    for dx in (0, 1):
        for dy in (1, 7, 2, 6, 3, 5, 4, 0):
            if dx == 0 and dy == 0:
                continue
            there = lax.rem(xlo + dx, 2) * RING + wrap(y + dy)
            i = dx * RING + dy
            send(
                copy(lambda: slice_of(chip, 1, z), l1_s.at[i], l1_r.at[i], l1_dev(dx, dy)),
                my_group <= there // GROUP,
            )

    def need(g):
        return g * GROUP <= chip

    def l1_wait(g):
        for p in range(g * GROUP, (g + 1) * GROUP):
            i = lax.rem(xlo + p // RING, 2) * RING + wrap(y - p % RING)
            arrive(
                copy(lambda: slice_of(p, 1, z), l1_s.at[i], l1_r.at[i], sibling),
                jnp.logical_and(need(g), chip != p),
            )

    def z_copy(g, way, s):
        sign = 1 if way == 0 else -1
        half = GROUP // 2
        p0, n = (g * GROUP, GROUP) if s < 4 else (g * GROUP + way * half, half)
        return lambda src: copy(
            lambda: slice_of(p0, n, wrap(z - sign * src)), z_s.at[way, g, s - 1], z_r.at[way, g, s - 1], z_next[way]
        )

    def z_send(g, s):
        for way in (0, 1):
            send(z_copy(g, way, s)(s - 1), need(g))

    def z_wait(g, s):
        for way in (0, 1):
            arrive(z_copy(g, way, s)(s), need(g))

    def z_step(g, s):
        z_wait(g, s)
        if s < 4:
            z_send(g, s + 1)
        else:
            send(
                copy(lambda: keys.at[pl.ds(g * GROUP, GROUP), core], ks_s.at[g], ks_r.at[g], sibling),
                need(g),
            )

    def group_wait(g):
        arrive(
            copy(lambda: keys.at[pl.ds(g * GROUP, GROUP), 1 - core], ks_s.at[g], ks_r.at[g], sibling),
            need(g),
        )

    arrays = (wq, uk, uv)
    ORDER = (0, -1, -2, -3, -4, 3, 2, 1)

    def piece(a, xl, slot, c):
        p = xl * RING + wrap(y + ORDER[slot])
        return lambda: arrays[a].at[p, c]

    def wy_copy(a, way, s, src_slot):
        return copy(piece(a, xlo, src_slot, core), wy_s.at[way, s - 1, a], wy_r.at[way, s - 1, a], y_next[way])

    def wx_copy(part, slot, xl):
        p = xl * RING + wrap(y + ORDER[slot])
        ref = (
            lambda: wq.at[p, core, pl.ds(0, 32), :],
            lambda: wq.at[p, core, pl.ds(32, 16), :],
            lambda: uk.at[p, core],
            lambda: uv.at[p, core],
        )[part]
        return copy(ref, wx_s.at[slot, part], wx_r.at[slot, part], x_up if part == 0 else x_down)

    def ws_copy(a, column, slot, c):
        xl = xlo if column == 0 else 1 - xlo
        i = column * 8 + slot
        return copy(piece(a, xl, slot, c), ws_s.at[i, a], ws_r.at[i, a], sibling)

    def spread(a, slot):
        for part in (0, 1) if a == 0 else (a + 1,):
            send(wx_copy(part, slot, xlo))
        send(ws_copy(a, 0, slot, core))

    def w_begin():
        for a in range(3):
            for way in (0, 1):
                send(wy_copy(a, way, 1, 0))
            spread(a, 0)

    def w_step(s):
        for way in (0, 1):
            slot = s if way == 0 else 8 - s
            for a in range(3):
                if s == 4 and (a == 0) != (way == 0):
                    continue
                arrive(wy_copy(a, way, s, slot))
                if s < 3 or (s == 3 and (a == 0) == (way == 0)):
                    send(wy_copy(a, way, s + 1, slot))
                spread(a, slot)

    def w_across(slot):
        for a in range(3):
            for part in (0, 1) if a == 0 else (a + 1,):
                arrive(wx_copy(part, slot, 1 - xlo))
            send(ws_copy(a, 1, slot, core))

    def w_have(a):
        for column in (0, 1):
            for slot in range(8):
                arrive(ws_copy(a, column, slot, 1 - core))

    def project():
        xx = x_ref[0]
        w = wq[...].reshape(CHIPS * 2 * 48, WQW)
        query = jnp.dot(xx, w, preferred_element_type=F32)
        lane = lax.broadcasted_iota(jnp.int32, (ROWS, 128), 1)
        row = lax.broadcasted_iota(jnp.int32, (ROWS, 128), 0)
        half = ROT // 2
        expo = (-2.0 / ROT) * lax.rem(lane, half).astype(F32)
        freq = jnp.exp(expo * jnp.log(F32(50000.0)))
        angle = (ctx * ROWS + row).astype(F32) * freq
        first = lax.rem(lane, ROT) < half
        cosine = jnp.cos(angle)
        sine = jnp.sin(angle)
        sine = jnp.where(first, -sine, sine)
        scale = F32((NOPE + ROT) ** -0.5)
        ukw = uk[...].reshape(LAT, UPW)
        for j in range(HEADS // 2):
            q = query[:, UPW + j * 128 : UPW + (j + 1) * 128]
            other = jnp.where(first, pltpu.roll(q, 128 - half, 1), pltpu.roll(q, half, 1))
            rot = ((q * cosine + other * sine) * scale).astype(F32)
            left = jnp.where(lane < ROT, rot, 0.0)
            right = jnp.where(lane < ROT, pltpu.roll(rot, ROT, 1), 0.0)
            for h, part in ((2 * j, left), (2 * j + 1, right)):
                nope = query[:, h * NOPE : (h + 1) * NOPE].astype(BF16)
                q_lat = lax.dot_general(
                    nope, ukw[:, h * NOPE : (h + 1) * NOPE], (((1,), (1,)), ((), ())), preferred_element_type=F32
                )
                qf[pl.ds(h * ROWS, ROWS), :LAT] = (q_lat * scale).astype(BF16)
                qf[pl.ds(h * ROWS, ROWS), LAT:] = part.astype(BF16)
        mx[...] = jnp.full_like(mx, LOW)
        tot[...] = jnp.zeros_like(tot)
        acc[...] = jnp.zeros_like(acc)

    BLK = 384

    def attend(j):
        kc = keys[pl.ds(CHUNK * j, CHUNK)].reshape(CHUNK * 2 * ROWS, KEYW)
        width = CHUNK * 2 * ROWS
        for r in range(QROWS // BLK):
            rows = pl.ds(r * BLK, BLK)
            s = lax.dot_general(qf[rows, :], kc, (((1,), (1,)), ((), ())), preferred_element_type=F32)
            t = ctx * ROWS + lax.rem(lax.broadcasted_iota(jnp.int32, (BLK, width), 0), ROWS)
            u = j * width + lax.broadcasted_iota(jnp.int32, (BLK, width), 1)
            s = jnp.where(u <= t, s, LOW)
            old = mx[rows, :]
            new = jnp.maximum(old, jnp.max(s, -1, keepdims=True))
            mx[rows, :] = new
            alpha = jnp.exp(old - new)
            parts = [jnp.exp(s[:, i * 128 : (i + 1) * 128] - new) for i in range(width // 128)]
            tot[rows, :] = tot[rows, :] * alpha + functools.reduce(jnp.add, parts)
            prob = jnp.concatenate([p.astype(BF16) for p in parts], -1)
            add = jnp.dot(prob, kc[:, :LAT], preferred_element_type=F32)
            acc[rows, :] = acc[rows, :] * jnp.concatenate([alpha] * (LAT // 128), -1) + add

    def attend_group(g):
        per = GROUP // CHUNK

        def body(j, _):
            @pl.when(CHUNK * j <= chip)
            def _():
                attend(j)

            return 0

        lax.fori_loop(g * per, (g + 1) * per, body, 0)

    def peak_copy(stage, k):
        if stage == 0:
            to = plane_dev(k)
        else:
            to = dev(dp, xlo, wrap(y + k), core, z)
        return lambda: pltpu.make_async_remote_copy(
            src_ref=pk.at[stage, 0], dst_ref=pk.at[stage, k], send_sem=pk_s.at[stage, k],
            recv_sem=pk_r.at[stage, k], device_id=to, device_id_type=MESH,
        )

    def peak_begin():
        for h in range(HEADS):
            pk[0, 0, h : h + 1, :] = jnp.max(mx[pl.ds(h * ROWS, ROWS), :], 0, keepdims=True)
        pk[0, 0, HEADS:, :] = jnp.full((8 - HEADS, 128), LOW, F32)
        for k in range(1, 8):
            send(peak_copy(0, k))

    def peak_next():
        for k in range(1, 8):
            arrive(peak_copy(0, k))
        pk[1, 0] = jnp.max(pk[0], 0)
        for k in range(1, 8):
            send(peak_copy(1, k))

    def finish():
        for k in range(1, 8):
            arrive(peak_copy(1, k))
        peak = jnp.max(pk[1], 0)
        for h in range(HEADS):
            limit = jnp.full((1, 128), tau_ref[h].astype(F32), F32)
            gamma = limit / jnp.maximum(peak[h : h + 1, :], limit)
            root = jnp.sqrt(gamma)
            nwq_ref[h, :, :NOPE] = (wq_ref[h, :, :NOPE].astype(F32) * root).astype(BF16)
            nwq_ref[h, :, NOPE:] = (wq_ref[h, :, NOPE:].astype(F32) * gamma[:, :ROT]).astype(BF16)
            nuk_ref[h] = (uk_ref[h].astype(F32) * root).astype(BF16)

    def output():
        uvw = uv[...].reshape(LAT, UPW)
        for h in range(HEADS):
            rows = pl.ds(h * ROWS, ROWS)
            total = jnp.sum(tot[rows, :], -1, keepdims=True)
            mixed = (acc[rows, :] / total).astype(BF16)
            att_ref[0, :, h * NOPE : (h + 1) * NOPE] = jnp.dot(
                mixed, uvw[:, h * NOPE : (h + 1) * NOPE], preferred_element_type=F32
            ).astype(BF16)

    w_begin()
    for g in (0, 1):
        l1_wait(g)
        z_send(g, 1)
    w_step(1)
    w_across(0)
    z_step(0, 1)
    z_step(1, 1)
    w_step(2)
    for slot in (1, 7):
        w_across(slot)
    z_step(0, 2)
    z_step(1, 2)
    w_step(3)
    for slot in (2, 6):
        w_across(slot)
    z_step(0, 3)
    for g in (2, 3):
        l1_wait(g)
    z_send(2, 1)
    z_step(1, 3)
    z_send(3, 1)
    w_step(4)
    for slot in (3, 5, 4):
        w_across(slot)
    z_step(0, 4)
    z_step(1, 4)
    z_step(2, 1)
    w_have(0)
    w_have(1)
    z_step(3, 1)
    project()
    z_step(2, 2)
    z_step(3, 2)
    group_wait(0)
    attend_group(0)
    z_step(2, 3)
    z_step(3, 3)
    group_wait(1)
    attend_group(1)
    z_step(2, 4)
    z_step(3, 4)
    group_wait(2)
    attend_group(2)
    group_wait(3)
    attend_group(3)
    peak_begin()
    w_have(2)
    output()
    peak_next()
    finish()
    for cond, make in sent:
        guarded(cond, lambda: make().wait_send())


def shards(query_latent_rows, latent, wq_b, key_up_weight, value_up_weight, tau):
    dma = pltpu.SemaphoreType.DMA
    vmem = pl.BlockSpec(memory_space=pltpu.VMEM)
    return pl.pallas_call(
        kernel,
        out_shape=(
            jax.ShapeDtypeStruct((1, ROWS, UPW), BF16),
            jax.ShapeDtypeStruct(wq_b.shape, BF16),
            jax.ShapeDtypeStruct(key_up_weight.shape, BF16),
        ),
        in_specs=[vmem] * 5 + [pl.BlockSpec(memory_space=pltpu.SMEM)],
        out_specs=(vmem,) * 3,
        scratch_shapes=[
            pltpu.VMEM((CHIPS, 2, 48, WQW), BF16),
            pltpu.VMEM((CHIPS, 2, 16, UPW), BF16),
            pltpu.VMEM((CHIPS, 2, 16, UPW), BF16),
            pltpu.VMEM((CHIPS, 2, ROWS, KEYW), BF16),
            pltpu.VMEM((QROWS, KEYW), BF16),
            pltpu.VMEM((QROWS, 128), F32),
            pltpu.VMEM((QROWS, 128), F32),
            pltpu.VMEM((QROWS, LAT), F32),
            pltpu.VMEM((2, 8, 8, 128), F32),
            dma((16,)), dma((16,)),
            dma((2, 4, 3)), dma((2, 4, 3)),
            dma((8, 4)), dma((8, 4)),
            dma((16, 3)), dma((16, 3)),
            dma((2, GROUPS, 4)), dma((2, GROUPS, 4)),
            dma((GROUPS,)), dma((GROUPS,)),
            dma((2, 8)), dma((2, 8)),
        ],
        compiler_params=pltpu.CompilerParams(
            collective_id=0, has_side_effects=True, vmem_limit_bytes=48 * 1024 * 1024
        ),
        name="latent_attention",
    )(query_latent_rows, latent, wq_b, key_up_weight, value_up_weight, tau)


def solution(mesh):
    in_specs = (
        P("dp", "ctx", None),
        P("dp", "ctx", None),
        P("head", "ctx", None),
        P("head", "ctx", None),
        P("head", "ctx", None),
        P("head"),
    )
    out_specs = (P("dp", "ctx", "head"), P("head", "ctx", None), P("head", "ctx", None))
    return jax.shard_map(shards, mesh=mesh, in_specs=in_specs, out_specs=out_specs, check_vma=False)
```

time: 323 us -> 82.4 us (0.26)
  blocking collectives: 201 us -> 0 us
  Pallas kernels: 0 us -> 77.5 us
  waiting for transfers between devices: 73.9 us -> 0 us
  matrix products: 21.7 us -> 0 us
  between operations: 14.2 us -> 0.71 us
  other arithmetic: 7.78 us -> 0 us
    pmax x1 -> x0, blocking collectives: 124 us -> none  [shards(): peak = lax.pmax(jnp.max(running, 0), ('dp', 'ctx'))]
    all_gather x2 -> x0, blocking collectives: 77.7 us -> none  [the longest x1 40 us: shards(): lax.all_gather(key_up_weight, 'ctx', axis=1, tiled=True)]
    pallas_call x0 -> x1, Pallas kernels: none -> 77.5 us  [shards(): pl.pallas_call(kernel, out_shape=(jax.ShapeDtypeStruct((1, ROWS, UPW), BF...]
    all_gather x2 -> x0, waiting for transfers between devices: 72.5 us -> none  [the longest x1 72.5 us: shards(): key_rows = lax.all_gather(latent, 'ctx', axis=1, tiled=True)[0]]
    dot_general x4 -> x0, matrix products: 21.7 us -> none  [the longest x1 9.58 us: shards(): jnp.einsum('euz,uzo->euo', mixed_output, value_up_rows, preferred_element...]
    reduce_sum x1 -> x0, other arithmetic: 3.92 us -> none  [shards(): totals = jnp.sum(exponent_terms, -1)]
  transfers between devices with their start and end apart: 2 -> 0, of which waited for: 1 -> 0; matrix products, arithmetic and copies ran while one was open for 2% -> 0% of each run, Pallas kernels for 0% -> 0%
where the time goes in v1:
time: 82.4 us; the launch traced here: 82.2 us
  Pallas kernels  77.5 us (94%)
  local copies, waits for them, and re-layouts  4.05 us (5%)
    pallas_call x1, Pallas kernels, shards(): pl.pallas_call(kernel, out_shape=(jax.ShapeDtypeStruct((1, ROWS, UPW), BF...  77.5 us
    unnamed x14, local copies, waits for them, and re-layouts  4.05 us

profile of v1, /device:TPU:1, one launch (start us, length us, event | category | flops | bytes accessed | tf_op | source)
XLA Modules:
  0.0 82.2 jit_solution(5439751893523281950)
XLA Ops:
  0.6 0.0 copy-start.4
  0.6 0.0 copy-start.3
  0.7 0.0 copy-start.2
  0.7 0.0 copy-start.1
  0.7 1.1 %copy.9.lat_ref = bf16[1,128,576]{2,1,0:T(8,128)(2,1)S(1)} copy(bf16[1,128,576]{1,2,0:T(8,128)(2,1)} %param.7) | data formatting | bytes 294912 | tf_op args[1]
  1.8 0.0 copy-done.4
  1.8 0.0 copy-done.3
  1.8 0.0 copy-done.2
  1.8 0.0 copy-done.1
  1.8 0.0 copy-start
  1.8 1.0 %copy-done = bf16[1,128,1536]{2,1,0:T(8,128)(2,1)S(1)} copy-done((bf16[1,128,1536]{2,1,0:T(8,128)(2,1)S(1)}, bf16[1,128,1536]{2,1,0:T(8,128)(2,1)}, u32[]{:S(2)}) %copy-start) | copy-done | bytes 393240
  2.8 77.5 %latent_attention.1 = (bf16[1,128,768]{2,1,0:T(8,128)(2,1)S(1)}, bf16[6,48,192]{2,1,0:T(8,128)(2,1)S(1)}, bf16[6,16,128]{2,1,0:T(8,128)(2,1)S(1)}) custom-call(bf16[1,128,1536]{2,1,0:T(8,128)(2,1)S(1)} %copy-done, bf16[1,128,576]{2,1,0:T(8,128)(2,1)S(1)} %copy.9.lat_ref, bf16[6,48,192]{2,1,0:T(8,128)(2,1)S(1)} %copy-done.1, ...), custom_call_target="tpu_custom_call" | custom-call | tf_op jit(solution)/shard_map/latent_attention/pallas_call | solution.py:395
  80.3 0.7 copy.13
  81.0 0.7 copy.14
  81.6 0.6 copy.15
Async XLA Ops:
  0.6 1.1 %copy-start.4 = (s32[6]{0:T(128)S(1)}, s32[6]{0:T(128)}, u32[]{:S(2)}) copy-start(s32[6]{0:T(128)} %tau_ref.1) | copy-start | bytes 76
  0.6 1.1 %copy-start.3 = (bf16[6,16,128]{2,1,0:T(8,128)(2,1)S(1)}, bf16[6,16,128]{2,1,0:T(8,128)(2,1)}, u32[]{:S(2)}) copy-start(bf16[6,16,128]{2,1,0:T(8,128)(2,1)} %uv_ref.1) | copy-start | bytes 73732
  0.7 1.1 %copy-start.2 = (bf16[6,16,128]{2,1,0:T(8,128)(2,1)S(1)}, bf16[6,16,128]{2,1,0:T(8,128)(2,1)}, u32[]{:S(2)}) copy-start(bf16[6,16,128]{2,1,0:T(8,128)(2,1)} %uk_ref.1) | copy-start | bytes 73732
  0.7 1.1 %copy-start.1 = (bf16[6,48,192]{2,1,0:T(8,128)(2,1)S(1)}, bf16[6,48,192]{2,1,0:T(8,128)(2,1)}, u32[]{:S(2)}) copy-start(bf16[6,48,192]{2,1,0:T(8,128)(2,1)} %wq_ref.1) | copy-start | bytes 331780
  1.8 1.0 %copy-start = (bf16[1,128,1536]{2,1,0:T(8,128)(2,1)S(1)}, bf16[1,128,1536]{2,1,0:T(8,128)(2,1)}, u32[]{:S(2)}) copy-start(bf16[1,128,1536]{2,1,0:T(8,128)(2,1)} %x_ref.1) | copy-start | bytes 1179652

commit v2 on v0

v2 whole, which is shorter than its diff:
```python
import functools

import jax
import jax.numpy as jnp
from jax import lax
from jax.experimental import pallas as pl
from jax.experimental.pallas import tpu as pltpu
from jax.sharding import PartitionSpec as P

MESH = pl.DeviceIdType.MESH
F32 = jnp.float32
BF16 = jnp.bfloat16
LOW = -1e30

HEADS = 6
HALF = 3
ROWS = 128
TOKS = 2 * ROWS
NOPE = 128
ROT = 64
LAT = 512
KEYW = LAT + ROT
RING = 8
CHIPS = 16
QUARTER = KEYW // 4
WROW = 48
UROW = 16
UPW = HALF * NOPE
WQW = UPW + 2 * 128
QROWS = HALF * TOKS
CHUNK = 2
WIDTH = CHUNK * TOKS
PLANE = 32


def kernel(
    x_ref, lat_ref, wq_ref, uk_ref, uv_ref, tau_ref,
    att_ref, nwq_ref, nuk_ref,
    wq, uk, uv, keys, xs, wq_in, uk_in, uv_in, wq_st, uk_st, uv_st, qf, score, mx, tot, acc, pk, pk2, att_out, att_in,
    ld_s, in_s, in_r, l1_s, l1_r, lx_s, wy_s, wy_r, wx_s, wx_r, z_s, z_r, ks_s, ks_r, pk_s, pk_r, fin_s, fin_r,
):
    dp = lax.axis_index("dp")
    ctx = lax.axis_index("ctx")
    z = lax.axis_index("head")
    core = lax.rem(ctx, 2)
    chip = ctx // 2
    xlo = chip // RING
    y = lax.rem(chip, RING)

    def wrap(v):
        return lax.rem(v + 2 * RING, RING)

    def dev(d, xl, yy, c, zz):
        return (d, (xl * RING + yy) * 2 + c, zz)

    sibling = dev(dp, xlo, y, 1 - core, z)
    y_next = (dev(dp, xlo, wrap(y + 1), core, z), dev(dp, xlo, wrap(y - 1), core, z))
    z_next = (dev(dp, xlo, y, core, wrap(z + 1)), dev(dp, xlo, y, core, wrap(z - 1)))
    def plane_dev(k):
        return dev(lax.rem(dp + k // 16, 2), lax.rem(xlo + (k // 8) % 2, 2), wrap(y + k % 8), core, z)

    def lay_out(c, wq_to, uk_to, uv_to):
        for i in range(HALF):
            h = HALF * c + i
            cols = slice(i * NOPE, (i + 1) * NOPE)
            wq_to[:, cols] = wq_in[h, :, :NOPE]
            uk_to[:, cols] = uk_in[h]
            uv_to[:, cols] = uv_in[h]
        rope = [wq_in[HALF * c + i, :, NOPE:] for i in range(HALF)]
        wq_to[:, UPW : UPW + 128] = jnp.concatenate(rope[:2], -1)
        wq_to[:, UPW + 128 :] = jnp.concatenate([rope[2], jnp.zeros((WROW, ROT), BF16)], -1)

    def wrows(c):
        return pl.ds(pl.multiple_of(c * WROW, WROW), WROW)

    def urows(c):
        return pl.ds(pl.multiple_of(c * UROW, UROW), UROW)


    def quarter(zz):
        return pl.ds(pl.multiple_of(lax.rem(zz + 8, 4) * QUARTER, QUARTER), QUARTER)

    loads = [
        pltpu.make_async_copy(wq_ref, wq_in, ld_s.at[0]),
        pltpu.make_async_copy(uk_ref, uk_in, ld_s.at[1]),
        pltpu.make_async_copy(uv_ref, uv_in, ld_s.at[2]),
        pltpu.make_async_copy(x_ref.at[0], xs.at[core], ld_s.at[3]),
        pltpu.make_async_copy(lat_ref.at[0], keys.at[chip, core], ld_s.at[4]),
    ]
    for load in loads:
        load.start()
    barrier = pltpu.get_barrier_semaphore()
    partners = [plane_dev(k) for d in (4, 3, 5, 2, 6, 1, 7, 0) for k in range(1, PLANE) if k % 8 == d]
    partners += [*z_next, sibling]
    for partner in partners:
        pl.semaphore_signal(barrier, inc=1, device_id=partner, device_id_type=MESH)
    for load in loads:
        load.wait()
    lay_out(1 - core, wq_st, uk_st, uv_st)
    lay_out(core, wq.at[chip, wrows(core)], uk.at[chip, urows(core)], uv.at[chip, urows(core)])
    pl.semaphore_wait(barrier, len(partners))

    sent = []

    def guarded(cond, f):
        if cond is None:
            f()
        else:
            pl.when(cond)(f)

    def send(make, cond=None):
        sent.append((cond, make))
        guarded(cond, lambda: make().start())

    def arrive(make, cond=None):
        guarded(cond, lambda: make().wait_recv())

    def copy(src, dst, ssem, rsem, to):
        return lambda: pltpu.make_async_remote_copy(
            src_ref=src(), dst_ref=dst(), send_sem=ssem, recv_sem=rsem, device_id=to, device_id_type=MESH
        )

    def in_copy(i, c):
        src, dst = (
            (lambda: wq_st, lambda: wq.at[chip, wrows(c)]),
            (lambda: uk_st, lambda: uk.at[chip, urows(c)]),
            (lambda: uv_st, lambda: uv.at[chip, urows(c)]),
            (lambda: xs.at[c], lambda: xs.at[c]),
        )[i]
        return copy(src, dst, in_s.at[i], in_r.at[i], sibling)

    ORDER = (0, -1, -2, -3, -4, 3, 2, 1)
    ACROSS = ((0, 0, 1, 1, 1, 1, 0, 1), (0, 1, 0, 1, 0, 1, 0, 1))

    def piece(a, xl, slot):
        p = xl * RING + wrap(y + ORDER[slot])
        if a < 6:
            src = core if a < 3 else 1 - core
            rows = pl.ds(pl.multiple_of(src * WROW + (a % 3) * 16, 16), 16)
            return lambda: wq.at[p, rows]
        return (lambda: uk.at[p]) if a == 6 else (lambda: uv.at[p])

    def wy_copy(a, way, s, slot):
        ref = piece(a, xlo, slot)
        return copy(ref, ref, wy_s.at[way, s - 1, a], wy_r.at[way, s - 1, a], y_next[way])

    def wx_copy(a, slot, xl, turn=0):
        ref = piece(a, xl, slot)
        down = jnp.where(xlo == 0, ACROSS[0][a], ACROSS[1][a])
        to = dev(lax.rem(dp + xlo + down, 2), 1 - xlo, wrap(y + turn), core, z)
        index = slot if turn == 0 else 4
        return copy(ref, ref, wx_s.at[index, a], wx_r.at[index, a], to)

    def w_begin(a):
        for way in (0, 1):
            send(wy_copy(a, way, 1, 0))
        send(wx_copy(a, 0, xlo))

    def w_step(s, parts=range(8)):
        for a in parts:
            for way in (0, 1):
                slot = s if way == 0 else 8 - s
                if s == 4 and a % 2 != way:
                    continue
                arrive(wy_copy(a, way, s, slot))
                if s < 3:
                    send(wy_copy(a, way, s + 1, slot))
                if s == 3 and a % 2 == way:
                    send(wx_copy(a, slot, xlo, 1 if way == 0 else -1))
                    send(wy_copy(a, way, s + 1, slot))
                if s < 4:
                    send(wx_copy(a, slot, xlo))

    def w_have(parts):
        for slot in range(8):
            for a in parts:
                arrive(wx_copy(a, slot, 1 - xlo))

    def keys_of(p, zz):
        return lambda: keys.at[p, core, quarter(zz), :]

    left = xlo == 0
    right = xlo == 1
    source = [chip] + [xlo * RING + wrap(y - k) for k in range(1, RING)] + list(range(RING))
    wanted = [None] + [y >= k for k in range(1, RING)] + [right] * RING

    def l1_copy(k):
        p = chip if k == 0 else source[k]
        return copy(keys_of(p, z), keys_of(p, z), l1_s.at[0], l1_r.at[k], plane_dev(8))

    def l1_begin():
        for k in (1, 7, 2, 6, 3, 5, 4):
            ref = keys_of(chip, z)
            send(
                copy(ref, ref, l1_s.at[k], l1_r.at[k], plane_dev(k)),
                jnp.logical_or(left, y + k < RING),
            )
        across(chip, left)

    def across(p, cond):
        ref = keys_of(p, z)
        i = 8 + lax.rem(p, RING)
        send(copy(ref, ref, lx_s.at[i - 8], l1_r.at[i], plane_dev(8)), cond)

    def l1_wait(k):
        arrive(l1_copy(k), jnp.logical_or(left, wanted[k]) if k < 8 else wanted[k])
        if k < 8:
            across(source[k], left)
        for way in (0, 1):
            send(z_copy(k, way, 1), wanted[k])

    def z_copy(k, way, s, src=None):
        sign = 1 if way == 0 else -1
        ref = keys_of(source[k], z - sign * (s - 1 if src is None else src))
        return copy(ref, ref, z_s.at[way, s - 1, k], z_r.at[way, s - 1, k], z_next[way])

    def z_turn(k):
        for way in (0, 1):
            arrive(z_copy(k, way, 1, 1), wanted[k])
        send(z_copy(k, k % 2, 2), wanted[k])

    def ks_copy(p, c):
        ref = lambda: keys.at[p, c]
        return copy(ref, ref, ks_s.at[p], ks_r.at[p], sibling)

    def z_end(k):
        if k:
            arrive(z_copy(k, k % 2, 2, 2), wanted[k])
        send(ks_copy(source[k], core), wanted[k])

    def chip_wait(p):
        arrive(ks_copy(p, 1 - core), p <= chip)

    def project():
        xx = xs[...].reshape(TOKS, 2 * CHIPS * WROW)
        w = wq[...].reshape(2 * CHIPS * WROW, WQW)
        query = jnp.dot(xx, w, preferred_element_type=F32)
        lane = lax.broadcasted_iota(jnp.int32, (TOKS, 128), 1)
        row = lax.broadcasted_iota(jnp.int32, (TOKS, 128), 0)
        half = ROT // 2
        expo = (-2.0 / ROT) * lax.rem(lane, half).astype(F32)
        freq = jnp.exp(expo * jnp.log(F32(50000.0)))
        angle = (chip * TOKS + row).astype(F32) * freq
        first = lax.rem(lane, ROT) < half
        cosine = jnp.cos(angle)
        sine = jnp.sin(angle)
        sine = jnp.where(first, -sine, sine)
        scale = F32((NOPE + ROT) ** -0.5)
        ukw = uk[...].reshape(LAT, UPW)
        rots = []
        for j in range(2):
            q = query[:, UPW + j * 128 : UPW + (j + 1) * 128]
            other = jnp.where(first, pltpu.roll(q, 128 - half, 1), pltpu.roll(q, half, 1))
            rots.append((q * cosine + other * sine) * scale)
        rots = [rots[0][:, :ROT], pltpu.roll(rots[0], ROT, 1)[:, :ROT], rots[1][:, :ROT]]
        for i in range(HALF):
            rows = pl.ds(i * TOKS, TOKS)
            nope = query[:, i * NOPE : (i + 1) * NOPE].astype(BF16)
            q_lat = lax.dot_general(
                nope, ukw[:, i * NOPE : (i + 1) * NOPE], (((1,), (1,)), ((), ())), preferred_element_type=F32
            )
            qf[rows, :LAT] = (q_lat * scale).astype(BF16)
            qf[rows, LAT:] = rots[i].astype(BF16)
        mx[...] = jnp.full_like(mx, LOW)

    def keys_at(j):
        at = [jnp.minimum(CHUNK * j + a, chip) for a in range(CHUNK)]
        return jnp.concatenate([keys[p, c] for p in at for c in range(2)], -1)

    def scores(j, masked):
        kt = keys_at(j)
        for i in range(HALF):
            rows = pl.ds(i * TOKS, TOKS)
            s = jnp.dot(qf[rows, :], kt, preferred_element_type=F32)
            if masked:
                t = (chip - CHUNK * j) * TOKS + lax.broadcasted_iota(jnp.int32, (TOKS, WIDTH), 0)
                s = jnp.where(lax.broadcasted_iota(jnp.int32, (TOKS, WIDTH), 1) <= t, s, LOW)
            score[j, rows, :] = s
            parts = [s[:, b * 128 : (b + 1) * 128] for b in range(WIDTH // 128)]
            mx[rows, :] = functools.reduce(jnp.maximum, parts, mx[rows, :])

    def scores_all():
        def body(j, _):
            for a in range(CHUNK):
                chip_wait(CHUNK * j + a)

            @pl.when(j < chip // CHUNK)
            def _():
                scores(j, False)

            @pl.when(j == chip // CHUNK)
            def _():
                scores(j, True)

            return 0

        lax.fori_loop(0, CHIPS // CHUNK, body, 0)

    def mix_all():
        mx[...] = jnp.broadcast_to(jnp.max(mx[...], -1, keepdims=True), mx.shape)
        tot[...] = jnp.zeros_like(tot)
        acc[...] = jnp.zeros_like(acc)

        def body(j, _):
            kt = keys_at(j)[:LAT]
            for i in range(HALF):
                rows = pl.ds(i * TOKS, TOKS)
                top = mx[rows, :]
                parts = [jnp.exp(score[j, rows, b * 128 : (b + 1) * 128] - top) for b in range(WIDTH // 128)]
                tot[rows, :] += functools.reduce(jnp.add, parts)
                prob = jnp.concatenate([p.astype(BF16) for p in parts], -1)
                acc[rows, :] += lax.dot_general(prob, kt, (((1,), (1,)), ((), ())), preferred_element_type=F32)
            return 0

        lax.fori_loop(0, chip // CHUNK + 1, body, 0)

    def peak_copy(k):
        return copy(lambda: pk.at[0], lambda: pk.at[k], pk_s.at[k], pk_r.at[k], plane_dev(k))

    def peak_begin():
        for i in range(HALF):
            pk[0, i : i + 1, :] = jnp.max(mx[pl.ds(i * TOKS, TOKS), :], 0, keepdims=True)
        pk[0, HALF:, :] = jnp.full((8 - HALF, 128), LOW, F32)
        for k in [k for d in (4, 3, 5, 2, 6, 1, 7, 0) for k in range(1, PLANE) if k % 8 == d]:
            send(peak_copy(k))

    def fin_copy(i, c):
        src, dst = (
            (lambda: pk2.at[c], lambda: pk2.at[c]),
            (lambda: att_out, lambda: att_in),
        )[i]
        return copy(src, dst, fin_s.at[i], fin_r.at[i], sibling)

    def peak_end():
        for k in range(1, PLANE):
            arrive(peak_copy(k))
        pk2[core] = jnp.max(pk[...], 0)
        send(fin_copy(0, core))

    def finish():
        arrive(fin_copy(0, 1 - core))
        for h in range(HEADS):
            peak = jnp.max(pk2[h // HALF, h % HALF : h % HALF + 1, :], -1, keepdims=True)
            limit = jnp.full((1, 128), tau_ref[h].astype(F32), F32)
            gamma = limit / jnp.maximum(peak, limit)
            root = jnp.sqrt(gamma)
            nwq_ref[h, :, :NOPE] = (wq_in[h, :, :NOPE].astype(F32) * root).astype(BF16)
            nwq_ref[h, :, NOPE:] = (wq_in[h, :, NOPE:].astype(F32) * gamma[:, :ROT]).astype(BF16)
            nuk_ref[h] = (uk_in[h].astype(F32) * root).astype(BF16)

    def output():
        uvw = uv[...].reshape(LAT, UPW)

        def of(c, i):
            rows = pl.ds(pl.multiple_of(i * TOKS + c * ROWS, ROWS), ROWS)
            total = jnp.sum(tot[rows, :], -1, keepdims=True)
            mixed = (acc[rows, :] / total).astype(BF16)
            w = uvw[:, i * NOPE : (i + 1) * NOPE]
            return jnp.dot(mixed, w, preferred_element_type=F32).astype(BF16)

        for i in range(HALF):
            att_out[:, i * NOPE : (i + 1) * NOPE] = of(1 - core, i)
        send(fin_copy(1, core))
        for i in range(HALF):
            att_ref[0, :, pl.ds(pl.multiple_of((core * HALF + i) * NOPE, NOPE), NOPE)] = of(core, i)

    def output_end():
        arrive(fin_copy(1, 1 - core))
        att_ref[0, :, pl.ds(pl.multiple_of((1 - core) * UPW, UPW), UPW)] = att_in[...]

    for i in range(4):
        send(in_copy(i, core))
    for a in range(3):
        w_begin(a)
    l1_begin()
    arrive(in_copy(0, 1 - core))
    for a in (3, 4, 5):
        w_begin(a)
    arrive(in_copy(1, 1 - core))
    w_begin(6)
    arrive(in_copy(2, 1 - core))
    w_begin(7)
    z_end(0)
    for k in (1, 7):
        l1_wait(k)
    w_step(1)
    for k in (2, 6, 3, 5, 4):
        l1_wait(k)
    w_step(2)
    for k in (1, 7, 2):
        z_turn(k)
    for k in range(8, 16):
        l1_wait(k)
    w_step(3)
    for k in (6, 3, 5, 4):
        z_turn(k)
    for k in (1, 7, 2, 6, 3):
        z_end(k)
    for k in (8, 9, 10, 11):
        z_turn(k)
    w_step(4)
    arrive(in_copy(3, 1 - core))
    for k in (12, 13, 14, 15):
        z_turn(k)
    for k in (5, 4, 8, 9, 10, 11):
        z_end(k)
    w_have(range(7))
    project()
    for k in (12, 13, 14, 15):
        z_end(k)
    scores_all()
    peak_begin()
    mix_all()
    w_have((7,))
    output()
    peak_end()
    output_end()
    finish()
    for cond, make in sent:
        guarded(cond, lambda: make().wait_send())


def shards(query_latent_rows, latent, wq_b, key_up_weight, value_up_weight, tau):
    dma = pltpu.SemaphoreType.DMA
    vmem = pl.BlockSpec(memory_space=pltpu.VMEM)
    hbm = pl.BlockSpec(memory_space=pltpu.HBM)
    return pl.pallas_call(
        kernel,
        out_shape=(
            jax.ShapeDtypeStruct((1, ROWS, HEADS * NOPE), BF16),
            jax.ShapeDtypeStruct(wq_b.shape, BF16),
            jax.ShapeDtypeStruct(key_up_weight.shape, BF16),
        ),
        in_specs=[hbm] * 5 + [pl.BlockSpec(memory_space=pltpu.SMEM)],
        out_specs=(vmem,) * 3,
        scratch_shapes=[
            pltpu.VMEM((CHIPS, 2 * WROW, WQW), BF16),
            pltpu.VMEM((CHIPS, 2 * UROW, UPW), BF16),
            pltpu.VMEM((CHIPS, 2 * UROW, UPW), BF16),
            pltpu.VMEM((CHIPS, 2, KEYW, ROWS), BF16),
            pltpu.VMEM((2, ROWS, 2 * CHIPS * WROW), BF16),
            pltpu.VMEM((HEADS, WROW, NOPE + ROT), BF16),
            pltpu.VMEM((HEADS, UROW, NOPE), BF16),
            pltpu.VMEM((HEADS, UROW, NOPE), BF16),
            pltpu.VMEM((WROW, WQW), BF16),
            pltpu.VMEM((UROW, UPW), BF16),
            pltpu.VMEM((UROW, UPW), BF16),
            pltpu.VMEM((QROWS, KEYW), BF16),
            pltpu.VMEM((CHIPS // CHUNK, QROWS, WIDTH), F32),
            pltpu.VMEM((QROWS, 128), F32),
            pltpu.VMEM((QROWS, 128), F32),
            pltpu.VMEM((QROWS, LAT), F32),
            pltpu.VMEM((PLANE, 8, 128), F32),
            pltpu.VMEM((2, 8, 128), F32),
            pltpu.VMEM((ROWS, UPW), BF16),
            pltpu.VMEM((ROWS, UPW), BF16),
            dma((5,)),
            dma((4,)), dma((4,)),
            dma((8,)), dma((16,)),
            dma((8,)),
            dma((2, 4, 8)), dma((2, 4, 8)),
            dma((8, 8)), dma((8, 8)),
            dma((2, 2, CHIPS)), dma((2, 2, CHIPS)),
            dma((CHIPS,)), dma((CHIPS,)),
            dma((PLANE,)), dma((PLANE,)),
            dma((2,)), dma((2,)),
        ],
        compiler_params=pltpu.CompilerParams(
            collective_id=0, has_side_effects=True, vmem_limit_bytes=63 * 1024 * 1024
        ),
        name="latent_attention",
    )(query_latent_rows, jnp.swapaxes(latent, 1, 2), wq_b, key_up_weight, value_up_weight, tau)


def solution(mesh):
    in_specs = (
        P("dp", "ctx", None),
        P("dp", "ctx", None),
        P("head", "ctx", None),
        P("head", "ctx", None),
        P("head", "ctx", None),
        P("head"),
    )
    out_specs = (P("dp", "ctx", "head"), P("head", "ctx", None), P("head", "ctx", None))
    return jax.shard_map(shards, mesh=mesh, in_specs=in_specs, out_specs=out_specs, check_vma=False)
```

time: 323 us -> 71.5 us (0.22)
  blocking collectives: 201 us -> 0 us
  waiting for transfers between devices: 73.9 us -> 0 us
  Pallas kernels: 0 us -> 67.6 us
  matrix products: 21.7 us -> 0 us
  between operations: 14.2 us -> 0.65 us
  other arithmetic: 7.78 us -> 0 us
    pmax x1 -> x0, blocking collectives: 124 us -> none  [shards(): peak = lax.pmax(jnp.max(running, 0), ('dp', 'ctx'))]
    all_gather x2 -> x0, blocking collectives: 77.7 us -> none  [the longest x1 40 us: shards(): lax.all_gather(key_up_weight, 'ctx', axis=1, tiled=True)]
    all_gather x2 -> x0, waiting for transfers between devices: 72.5 us -> none  [the longest x1 72.5 us: shards(): key_rows = lax.all_gather(latent, 'ctx', axis=1, tiled=True)[0]]
    pallas_call x0 -> x1, Pallas kernels: none -> 67.6 us  [shards(): pl.pallas_call(kernel, out_shape=(jax.ShapeDtypeStruct((1, ROWS, HEADS *...]
    dot_general x4 -> x0, matrix products: 21.7 us -> none  [the longest x1 9.58 us: shards(): jnp.einsum('euz,uzo->euo', mixed_output, value_up_rows, preferred_element...]
    reduce_sum x1 -> x0, other arithmetic: 3.92 us -> none  [shards(): totals = jnp.sum(exponent_terms, -1)]
  transfers between devices with their start and end apart: 2 -> 0, of which waited for: 1 -> 0; matrix products, arithmetic and copies ran while one was open for 2% -> 0% of each run, Pallas kernels for 0% -> 0%
where the time goes in v2:
time: 71.5 us; the launch traced here: 71.3 us
  Pallas kernels  67.6 us (95%)
  local copies, waits for them, and re-layouts  3 us (4%)
    pallas_call x1, Pallas kernels, shards(): pl.pallas_call(kernel, out_shape=(jax.ShapeDtypeStruct((1, ROWS, HEADS *...  67.6 us
    unnamed x7, local copies, waits for them, and re-layouts  3 us

profile of v2, /device:TPU:1, one launch (start us, length us, event | category | flops | bytes accessed | tf_op | source)
XLA Modules:
  0.0 71.3 jit_solution(18294394835211469790)
XLA Ops:
  0.6 67.6 %latent_attention.1 = (bf16[1,128,768]{2,1,0:T(8,128)(2,1)}, bf16[6,48,192]{2,1,0:T(8,128)(2,1)}, bf16[6,16,128]{2,1,0:T(8,128)(2,1)}) custom-call(bf16[1,128,1536]{2,1,0:T(8,128)(2,1)} %x_ref.1, bf16[1,576,128]{2,1,0:T(8,128)(2,1)} %bitcast.1, bf16[6,48,192]{2,1,0:T(8,128)(2,1)} %wq_ref.1, bf16[6,16,128]{2,1,0:T(8,128)(2,1)} %uk_ref.1, ...), custom_call_target="tpu_custom_call" | custom-call | tf_op jit(solution)/shard_map/latent_attention/pallas_call | solution.py:427
  68.3 0.0 copy-start
  68.3 1.7 %copy.12 = bf16[1,128,768]{2,1,0:T(8,128)(2,1)} copy(bf16[1,128,768]{2,1,0:T(8,128)(2,1)} %get-tuple-element.6) | data formatting | bytes 393216
  69.9 0.0 copy-done
  69.9 0.0 copy-start.1
  69.9 0.7 copy.13
  70.6 0.1 copy-done.1
  70.7 0.6 copy.14
Async XLA Ops:
  68.3 1.7 %copy-start = (bf16[6,48,192]{2,1,0:T(8,128)(2,1)S(1)}, bf16[6,48,192]{2,1,0:T(8,128)(2,1)}, u32[]{:S(2)}) copy-start(bf16[6,48,192]{2,1,0:T(8,128)(2,1)} %get-tuple-element.7) | copy-start | bytes 331780
  69.9 0.7 %copy-start.1 = (bf16[6,16,128]{2,1,0:T(8,128)(2,1)S(1)}, bf16[6,16,128]{2,1,0:T(8,128)(2,1)}, u32[]{:S(2)}) copy-start(bf16[6,16,128]{2,1,0:T(8,128)(2,1)} %get-tuple-element.8) | copy-start | bytes 73732

commit v3 on v2

--- a/solution.py
+++ b/solution.py
@@ -36,7 +36,7 @@
 def kernel(
     x_ref, lat_ref, wq_ref, uk_ref, uv_ref, tau_ref,
     att_ref, nwq_ref, nuk_ref,
-    wq, uk, uv, keys, xs, wq_in, uk_in, uv_in, wq_st, uk_st, uv_st, qf, score, mx, tot, acc, pk, pk2, att_out, att_in,
+    wq, uk, uv, keys, xs, wq_in, uk_in, uv_in, wq_st, uk_st, uv_st, qf, table, score, mx, tot, acc, pk, pk2, att_out, att_in,
     ld_s, in_s, in_r, l1_s, l1_r, lx_s, wy_s, wy_r, wx_s, wx_r, z_s, z_r, ks_s, ks_r, pk_s, pk_r, fin_s, fin_r,
 ):
     dp = lax.axis_index("dp")
@@ -221,7 +221,7 @@
 
     def ks_copy(p, c):
         ref = lambda: keys.at[p, c]
-        return copy(ref, ref, ks_s.at[p], ks_r.at[p], sibling)
+        return lambda: copy(ref, ref, ks_s.at[p], ks_r.at[p], sibling)()
 
     def z_end(k):
         if k:
@@ -231,20 +231,31 @@
     def chip_wait(p):
         arrive(ks_copy(p, 1 - core), p <= chip)
 
+    half = ROT // 2
+
+    def first_half():
+        return lax.rem(lax.broadcasted_iota(jnp.int32, (TOKS, 128), 1), ROT) < half
+
+    def prepare():
+        lane = lax.broadcasted_iota(jnp.int32, (TOKS, 128), 1)
+        row = lax.broadcasted_iota(jnp.int32, (TOKS, 128), 0)
+        expo = (-2.0 / ROT) * lax.rem(lane, half).astype(F32)
+        freq = jnp.exp(expo * jnp.log(F32(50000.0)))
+        angle = (chip * TOKS + row).astype(F32) * freq
+        sine = jnp.sin(angle)
+        table[0] = jnp.cos(angle)
+        table[1] = jnp.where(first_half(), -sine, sine)
+        mx[...] = jnp.full_like(mx, LOW)
+        tot[...] = jnp.zeros_like(tot)
+        acc[...] = jnp.zeros_like(acc)
+
     def project():
         xx = xs[...].reshape(TOKS, 2 * CHIPS * WROW)
         w = wq[...].reshape(2 * CHIPS * WROW, WQW)
         query = jnp.dot(xx, w, preferred_element_type=F32)
-        lane = lax.broadcasted_iota(jnp.int32, (TOKS, 128), 1)
-        row = lax.broadcasted_iota(jnp.int32, (TOKS, 128), 0)
-        half = ROT // 2
-        expo = (-2.0 / ROT) * lax.rem(lane, half).astype(F32)
-        freq = jnp.exp(expo * jnp.log(F32(50000.0)))
-        angle = (chip * TOKS + row).astype(F32) * freq
-        first = lax.rem(lane, ROT) < half
-        cosine = jnp.cos(angle)
-        sine = jnp.sin(angle)
-        sine = jnp.where(first, -sine, sine)
+        first = first_half()
+        cosine = table[0]
+        sine = table[1]
         scale = F32((NOPE + ROT) ** -0.5)
         ukw = uk[...].reshape(LAT, UPW)
         rots = []
@@ -261,7 +272,6 @@
             )
             qf[rows, :LAT] = (q_lat * scale).astype(BF16)
             qf[rows, LAT:] = rots[i].astype(BF16)
-        mx[...] = jnp.full_like(mx, LOW)
 
     def keys_at(j):
         at = [jnp.minimum(CHUNK * j + a, chip) for a in range(CHUNK)]
@@ -279,8 +289,17 @@
             parts = [s[:, b * 128 : (b + 1) * 128] for b in range(WIDTH // 128)]
             mx[rows, :] = functools.reduce(jnp.maximum, parts, mx[rows, :])
 
-    def scores_all():
-        def body(j, _):
+    def scores_all(events):
+        steps = CHIPS // CHUNK
+
+        def body(i, _):
+            for at, slots in events.items():
+                @pl.when(i == at)
+                def _():
+                    for k in slots:
+                        z_end(k)
+
+            j = lax.rem(i + xlo * (steps // 2), steps)
             for a in range(CHUNK):
                 chip_wait(CHUNK * j + a)
 
@@ -294,12 +313,10 @@
 
             return 0
 
-        lax.fori_loop(0, CHIPS // CHUNK, body, 0)
+        lax.fori_loop(0, steps, body, 0)
 
     def mix_all():
         mx[...] = jnp.broadcast_to(jnp.max(mx[...], -1, keepdims=True), mx.shape)
-        tot[...] = jnp.zeros_like(tot)
-        acc[...] = jnp.zeros_like(acc)
 
         def body(j, _):
             kt = keys_at(j)[:LAT]
@@ -370,9 +387,9 @@
 
     for i in range(4):
         send(in_copy(i, core))
+    l1_begin()
     for a in range(3):
         w_begin(a)
-    l1_begin()
     arrive(in_copy(0, 1 - core))
     for a in (3, 4, 5):
         w_begin(a)
@@ -381,34 +398,25 @@
     arrive(in_copy(2, 1 - core))
     w_begin(7)
     z_end(0)
-    for k in (1, 7):
+    prepare()
+    for k in (1, 7, 2, 6, 3, 5, 4):
         l1_wait(k)
-    w_step(1)
-    for k in (2, 6, 3, 5, 4):
-        l1_wait(k)
-    w_step(2)
-    for k in (1, 7, 2):
-        z_turn(k)
+    w_step(1, range(8))
     for k in range(8, 16):
         l1_wait(k)
-    w_step(3)
-    for k in (6, 3, 5, 4):
+    w_step(2, range(8))
+    for k in (1, 7, 2, 6, 3, 5, 4):
         z_turn(k)
-    for k in (1, 7, 2, 6, 3):
+    w_step(3, range(8))
+    for k in range(8, 16):
+        z_turn(k)
+    for k in (1, 7, 2, 6, 3, 5, 4):
         z_end(k)
-    for k in (8, 9, 10, 11):
-        z_turn(k)
-    w_step(4)
     arrive(in_copy(3, 1 - core))
-    for k in (12, 13, 14, 15):
-        z_turn(k)
-    for k in (5, 4, 8, 9, 10, 11):
-        z_end(k)
+    w_step(4, range(8))
     w_have(range(7))
     project()
-    for k in (12, 13, 14, 15):
-        z_end(k)
-    scores_all()
+    scores_all({1: (8, 9, 10, 11), 3: (12, 13, 14, 15)})
     peak_begin()
     mix_all()
     w_have((7,))
@@ -420,17 +428,24 @@
         guarded(cond, lambda: make().wait_send())
 
 
+def hand_over(a_ref, b_ref, c_ref, a_out, b_out, c_out):
+    a_out[...] = a_ref[...]
+    b_out[...] = b_ref[...]
+    c_out[...] = c_ref[...]
+
+
 def shards(query_latent_rows, latent, wq_b, key_up_weight, value_up_weight, tau):
     dma = pltpu.SemaphoreType.DMA
+    shapes = (
+        jax.ShapeDtypeStruct((1, ROWS, HEADS * NOPE), BF16),
+        jax.ShapeDtypeStruct(wq_b.shape, BF16),
+        jax.ShapeDtypeStruct(key_up_weight.shape, BF16),
+    )
     vmem = pl.BlockSpec(memory_space=pltpu.VMEM)
     hbm = pl.BlockSpec(memory_space=pltpu.HBM)
-    return pl.pallas_call(
+    made = pl.pallas_call(
         kernel,
-        out_shape=(
-            jax.ShapeDtypeStruct((1, ROWS, HEADS * NOPE), BF16),
-            jax.ShapeDtypeStruct(wq_b.shape, BF16),
-            jax.ShapeDtypeStruct(key_up_weight.shape, BF16),
-        ),
+        out_shape=shapes,
         in_specs=[hbm] * 5 + [pl.BlockSpec(memory_space=pltpu.SMEM)],
         out_specs=(vmem,) * 3,
         scratch_shapes=[
@@ -446,6 +461,7 @@
             pltpu.VMEM((UROW, UPW), BF16),
             pltpu.VMEM((UROW, UPW), BF16),
             pltpu.VMEM((QROWS, KEYW), BF16),
+            pltpu.VMEM((2, TOKS, 128), F32),
             pltpu.VMEM((CHIPS // CHUNK, QROWS, WIDTH), F32),
             pltpu.VMEM((QROWS, 128), F32),
             pltpu.VMEM((QROWS, 128), F32),
@@ -470,6 +486,13 @@
         ),
         name="latent_attention",
     )(query_latent_rows, jnp.swapaxes(latent, 1, 2), wq_b, key_up_weight, value_up_weight, tau)
+    return pl.pallas_call(
+        hand_over,
+        out_shape=shapes,
+        in_specs=[vmem] * 3,
+        out_specs=(vmem,) * 3,
+        name="hand_over",
+    )(*made)
 
 
 def solution(mesh):

time: 71.5 us -> 65.1 us (0.910)
  Pallas kernels: 67.6 us -> 64.3 us
  local copies, waits for them, and re-layouts: 3 us -> 0 us
    pallas_call x1 -> x2, Pallas kernels: 67.6 us -> 64.3 us  [the longest x1 62.6 us: shards(): pl.pallas_call(kernel, out_shape=shapes, in_specs=[hbm] * 5 + [pl.BlockSp...]
    unnamed x7 -> x0, local copies, waits for them, and re-layouts: 3 us -> none
where the time goes in v3:
time: 65.1 us; the launch traced here: 65 us
  Pallas kernels  64.3 us (99%)
    pallas_call x1, Pallas kernels, shards(): pl.pallas_call(kernel, out_shape=shapes, in_specs=[hbm] * 5 + [pl.BlockSp...  62.6 us
    pallas_call x1, Pallas kernels, shards(): pl.pallas_call(hand_over, out_shape=shapes, in_specs=[vmem] * 3, out_spec...  1.74 us

profile of v3, /device:TPU:1, one launch (start us, length us, event | category | flops | bytes accessed | tf_op | source)
XLA Modules:
  0.0 65.0 jit_solution(13573330621538648216)
XLA Ops:
  0.6 62.6 %latent_attention.1 = (bf16[1,128,768]{2,1,0:T(8,128)(2,1)}, bf16[6,48,192]{2,1,0:T(8,128)(2,1)}, bf16[6,16,128]{2,1,0:T(8,128)(2,1)}) custom-call(bf16[1,128,1536]{2,1,0:T(8,128)(2,1)} %x_ref.1, bf16[1,576,128]{2,1,0:T(8,128)(2,1)} %bitcast.1, bf16[6,48,192]{2,1,0:T(8,128)(2,1)} %wq_ref.1, bf16[6,16,128]{2,1,0:T(8,128)(2,1)} %uk_ref.1, ...), custom_call_target="tpu_custom_call" | custom-call | tf_op jit(solution)/shard_map/latent_attention/pallas_call | solution.py:446
  63.2 1.7 %hand_over.1 = (bf16[1,128,768]{2,1,0:T(8,128)(2,1)}, bf16[6,48,192]{2,1,0:T(8,128)(2,1)}, bf16[6,16,128]{2,1,0:T(8,128)(2,1)}) custom-call(bf16[1,128,768]{2,1,0:T(8,128)(2,1)} %get-tuple-element.6.a_ref, bf16[6,48,192]{2,1,0:T(8,128)(2,1)} %get-tuple-element.7.b_ref, bf16[6,16,128]{2,1,0:T(8,128)(2,1)} %get-tuple-element.8.c_ref), custom_call_target="tpu_custom_call" | custom-call | tf_op jit(solution)/shard_map/hand_over/pallas_call | solution.py:489

commit v4 on v3

--- a/solution.py
+++ b/solution.py
@@ -111,6 +111,11 @@
     def send(make, cond=None):
         sent.append((cond, make))
         guarded(cond, lambda: make().start())
+
+    def drain(upto):
+        for cond, make in sent[:upto]:
+            guarded(cond, lambda: make().wait_send())
+        del sent[:upto]
 
     def arrive(make, cond=None):
         guarded(cond, lambda: make().wait_recv())
@@ -402,9 +407,10 @@
     for k in (1, 7, 2, 6, 3, 5, 4):
         l1_wait(k)
     w_step(1, range(8))
-    for k in range(8, 16):
-        l1_wait(k)
-    w_step(2, range(8))
+    for a in range(8):
+        l1_wait(8 + a)
+        w_step(2, (a,))
+    early = len(sent)
     for k in (1, 7, 2, 6, 3, 5, 4):
         z_turn(k)
     w_step(3, range(8))
@@ -414,6 +420,7 @@
         z_end(k)
     arrive(in_copy(3, 1 - core))
     w_step(4, range(8))
+    drain(early)
     w_have(range(7))
     project()
     scores_all({1: (8, 9, 10, 11), 3: (12, 13, 14, 15)})
@@ -421,11 +428,11 @@
     mix_all()
     w_have((7,))
     output()
+    drain(len(sent) - 1)
     peak_end()
     output_end()
     finish()
-    for cond, make in sent:
-        guarded(cond, lambda: make().wait_send())
+    drain(len(sent))
 
 
 def hand_over(a_ref, b_ref, c_ref, a_out, b_out, c_out):

time: 65.1 us -> 64.9 us (level)
  no operation moved by 1% of the time
where the time goes in v4:
time: 64.9 us; the launch traced here: 64.8 us
  Pallas kernels  64.1 us (99%)
    pallas_call x1, Pallas kernels, shards(): pl.pallas_call(kernel, out_shape=shapes, in_specs=[hbm] * 5 + [pl.BlockSp...  62.4 us
    pallas_call x1, Pallas kernels, shards(): pl.pallas_call(hand_over, out_shape=shapes, in_specs=[vmem] * 3, out_spec...  1.74 us

profile of v4, /device:TPU:1, one launch (start us, length us, event | category | flops | bytes accessed | tf_op | source)
XLA Modules:
  0.0 64.8 jit_solution(842789768066877884)
XLA Ops:
  0.6 62.4 %latent_attention.1 = (bf16[1,128,768]{2,1,0:T(8,128)(2,1)}, bf16[6,48,192]{2,1,0:T(8,128)(2,1)}, bf16[6,16,128]{2,1,0:T(8,128)(2,1)}) custom-call(bf16[1,128,1536]{2,1,0:T(8,128)(2,1)} %x_ref.1, bf16[1,576,128]{2,1,0:T(8,128)(2,1)} %bitcast.1, bf16[6,48,192]{2,1,0:T(8,128)(2,1)} %wq_ref.1, bf16[6,16,128]{2,1,0:T(8,128)(2,1)} %uk_ref.1, ...), custom_call_target="tpu_custom_call" | custom-call | tf_op jit(solution)/shard_map/latent_attention/pallas_call | solution.py:453
  63.0 1.7 %hand_over.1 = (bf16[1,128,768]{2,1,0:T(8,128)(2,1)}, bf16[6,48,192]{2,1,0:T(8,128)(2,1)}, bf16[6,16,128]{2,1,0:T(8,128)(2,1)}) custom-call(bf16[1,128,768]{2,1,0:T(8,128)(2,1)} %get-tuple-element.6.a_ref, bf16[6,48,192]{2,1,0:T(8,128)(2,1)} %get-tuple-element.7.b_ref, bf16[6,16,128]{2,1,0:T(8,128)(2,1)} %get-tuple-element.8.c_ref), custom_call_target="tpu_custom_call" | custom-call | tf_op jit(solution)/shard_map/hand_over/pallas_call | solution.py:496
